TPU v7x, 32 devices: a whole 2x2x4 slice. The times are simulated.
32 devices in a mesh: member: 2 (over y), tile: 4 (over z), tm: 2 (over x), level: 2 (over core).
Axes of the slice: x: 2, y: 2, z: 4, core: 2. Of those that a mesh axis runs over, the one named last changes fastest.
Arguments:
- control: float32 [32, 64, 1536], P(('member', 'level'), ('tile', 'tm')), parts along dimension 0, may hold values from -6 to 6
- residual: float32 [32, 64, 1536], P(('member', 'level'), ('tile', 'tm')), parts along dimension 0, may hold values from -6 to 6
- direction: float32 [32, 64, 1536], P(('member', 'level'), ('tile', 'tm')), parts along dimension 0, may hold values from -6 to 6
- sigma: float32 [32, 64, 1536], P(('member', 'level'), ('tile', 'tm')), parts along dimension 0, may hold values from 0.3 to 3
- decay_rate: float32 [32], P(('member', 'level')), parts along dimension 0, may hold values from 0.005 to 0.4
- obs_cell: int32 [32, 8, 128], P(('member', 'tile'), 'tm'), parts along dimension 0, may hold values from 0 to 23039
- observation_slot: int32 [32, 8, 128], P(('member', 'tile'), 'tm'), parts along dimension 0, may hold values from 0 to 23
- block_count: int32 [32, 8], P(('member', 'tile'), 'tm'), parts along dimension 0, may hold values from 1 to 128, as said below
- horiz_weight: float32 [32, 8, 4, 128], P(('member', 'tile'), 'tm'), parts along dimension 0, may hold values from 0.05 to 0.45
- vert_weight: float32 [32, 8, 16, 128], P(('member', 'tile'), 'tm', 'level'), parts along dimension 0, may hold values from -2.4 to 2.4
- obs_precision: float32 [32, 8, 128], P(('member', 'tile'), 'tm'), parts along dimension 0, may hold values from 2 to 8
Outputs:
- control_new: float32 [32, 64, 1536], P(('member', 'level'), ('tile', 'tm')), parts along dimension 0
- residual_new: float32 [32, 64, 1536], P(('member', 'level'), ('tile', 'tm')), parts along dimension 0
- updated_direction: float32 [32, 64, 1536], P(('member', 'level'), ('tile', 'tm')), parts along dimension 0
There are 2 independent parts, one for each index of `member`. A program takes and returns all parts, laid end to end along the dimension named above; each array names one. Nothing has to cross between parts.
Inputs may be any that keep to these rules, and one draw needn't show every extreme that they name: `block_count`: every first block of each (a) row, b = 0, is full with 128 rows.
All inputs are finite; a program needn't handle non-finite values.
Results may differ from a plain program's by a relative error of at most 0.000024.
Values sent between devices are 32-bit elements; how exact they have to be, the bound alone decides.
A program may use at most 128 MiB of HBM per device.

v0:
```python
import jax
import jax.numpy as jnp
from jax import lax
from jax.sharding import PartitionSpec as P

K_DIFF = 4


center_coef = 0.1
row_coef = 0.2
level_coef = 0.05


def padded_2(block, sides, width):
    for axis, dim in sides:
        count = lax.axis_size(axis)
        forward = [(i, i + 1) for i in range(count - 1)]
        backward = [(target, source) for source, target in forward]
        low = lax.ppermute(
            lax.slice_in_dim(block, block.shape[dim] - width, None, axis=dim), axis, forward
        )
        high = lax.ppermute(lax.slice_in_dim(block, 0, width, axis=dim), axis, backward)
        block = jnp.concatenate([low, block, high], axis=dim)
    return block


def smooth(field):
    for step in range(K_DIFF):
        padded = padded_2(field, ((("tile", "tm"), 1), ("level", 0)), 1)
        rows_sum = (
            padded[1:-1, :-2] + padded[1:-1, 2:] + jnp.roll(field, 1, 2) + jnp.roll(field, -1, 2)
        )
        levels_sum = padded[:-2, 1:-1] + padded[2:, 1:-1]
        field = center_coef * field + row_coef * rows_sum + level_coef * levels_sum
    return field


def corners(cell, width):
    row = cell // width
    col = cell % width
    right = (col + 1) % width
    first = row * width
    return (first + col, first + right, first + width + col, first + width + right)


def local(
    control,
    residual,
    direction,
    sigma,
    decay_rate,
    obs_cell,
    observation_slot,
    block_count,
    horiz_weight,
    vert_weight,
    obs_precision,
):
    levels, rows, width = direction.shape
    weights_h, weights_v, precision = (
        lax.all_to_all(horiz_weight, "tile", split_axis=0, concat_axis=0, tiled=True),
        lax.all_to_all(vert_weight, "tile", split_axis=0, concat_axis=0, tiled=True),
        lax.all_to_all(obs_precision, "tile", split_axis=0, concat_axis=0, tiled=True),
    )
    cell, slot, counts = (
        lax.all_to_all(obs_cell, "tile", split_axis=0, concat_axis=0, tiled=True),
        lax.all_to_all(observation_slot, "tile", split_axis=0, concat_axis=0, tiled=True),
        lax.all_to_all(block_count, "tile", split_axis=0, concat_axis=0, tiled=True),
    )
    increment = sigma * smooth(direction)
    tile_field = lax.all_gather(increment, "tm", axis=1, tiled=True)
    flat = tile_field.reshape(levels, -1)
    cells = corners(cell, width)
    eff_weight = weights_v * jnp.exp(
        -slot[:, :, None, :].astype(jnp.float32) * decay_rate[None, None, :, None]
    )
    inner = jnp.zeros((levels,) + cell.shape, jnp.float32)
    for k in range(4):
        inner = inner + weights_h[:, :, k, :][None] * flat[:, cells[k]]
    partial_obs = jnp.sum(eff_weight * jnp.moveaxis(inner, 0, 2), axis=2)
    model_obs = lax.psum(partial_obs, "level")
    valid = jnp.arange(128, dtype=jnp.int32)[None, None, :] < counts[:, :, None]
    innovation_misfit = jnp.where(valid, precision * model_obs, 0.0)
    scaled = eff_weight * innovation_misfit[:, :, None, :]
    moved = jnp.moveaxis(scaled, 2, 0)
    tile_adjoint = jnp.zeros_like(flat)
    for k in range(4):
        values = (moved * weights_h[:, :, k, :][None]).reshape(levels, -1)
        tile_adjoint = tile_adjoint.at[:, cells[k].reshape(-1)].add(values)
    adjoint = lax.psum_scatter(
        tile_adjoint.reshape(tile_field.shape), "tm", scatter_dimension=1, tiled=True
    )
    image = direction + smooth(sigma * adjoint)
    norm_old, curvature, cross, image_norm = lax.psum(
        (
            jnp.sum(residual * residual),
            jnp.sum(direction * image),
            jnp.sum(residual * image),
            jnp.sum(image * image),
        ),
        ("tile", "tm", "level"),
    )
    alpha = norm_old / curvature
    residual_new = residual - alpha * image
    norm_new = norm_old - 2.0 * alpha * cross + alpha * alpha * image_norm
    control_new = control + alpha * direction
    updated_direction = residual_new + norm_new / norm_old * direction
    return (control_new, residual_new, updated_direction)


def solution(mesh):
    placed = (
        P(("member", "level"), ("tile", "tm"), None),
        P(("member", "level"), ("tile", "tm"), None),
        P(("member", "level"), ("tile", "tm"), None),
        P(("member", "level"), ("tile", "tm"), None),
        P(("member", "level")),
        P(("member", "tile"), "tm", None),
        P(("member", "tile"), "tm", None),
        P(("member", "tile"), "tm"),
        P(("member", "tile"), "tm", None, None),
        P(("member", "tile"), "tm", "level", None),
        P(("member", "tile"), "tm", None),
    )
    return jax.shard_map(
        local,
        mesh=mesh,
        in_specs=placed,
        out_specs=(
            P(("member", "level"), ("tile", "tm"), None),
            P(("member", "level"), ("tile", "tm"), None),
            P(("member", "level"), ("tile", "tm"), None),
        ),
        check_vma=False,
    )
```

profile of v0, /device:TPU:0, one launch (start us, length us, event | category | flops | bytes accessed | tf_op | source)
XLA Modules:
  0.0 376.2 jit_solution(16286580102609087812)
XLA Ops:
  8.4 4.8 %collective-permute-start = (f32[8,1,1536]{2,1,0:T(1,128)S(1)}, f32[8,1,1536]{2,1,0:T(1,128)S(1)}, u32[]{:S(2)}, u32[]{:S(2)}) collective-permute-start(f32[8,1,1536]{2,1,0:T(1,128)S(1)} %get-tuple-element.86), channel_id=1, source_target_pairs={{0,2},{2,4},{4,6},{6,8},{8,10},{10,12},{12,14},{1,3},{3,5},{5,7},{... | collective-permute-start | bytes 147464 | tf_op jit(solution)/shard_map/ppermute | solution.py:19
  14.6 6.9 %all-to-all-start = ((s32[4,4,128]{2,1,0:T(4,128)}), s32[4,4,128]{2,1,0:T(4,128)S(1)}, u32[]{:S(2)}, u32[]{:S(2)}) async-start(s32[4,4,128]{2,1,0:T(4,128)} %param.16), calls=%async_computation | async-start | bytes 16384 | tf_op jit(solution)/shard_map/all_to_all | solution.py:66
  23.7 3.4 all-to-all-done
  27.1 3.2 all-to-all-start.2
  31.7 4.2 %all-to-all-done.2 = s32[4,4,128]{2,1,0:T(4,128)S(1)} async-done(((s32[4,4,128]{2,1,0:T(4,128)}), s32[4,4,128]{2,1,0:T(4,128)S(1)}, u32[]{:S(2)}, u32[]{:S(2)}) %all-to-all-start.2) | async-done | bytes 8224 | tf_op jit(solution)/shard_map/all_to_all | solution.py:67
  35.9 3.3 all-to-all-start.5
  44.8 3.2 all-to-all-start.3
  54.5 5.1 %collective-permute-done.5 = f32[8,1,1536]{2,1,0:T(1,128)S(1)} collective-permute-done((f32[8,1,1536]{2,1,0:T(1,128)S(1)}, f32[8,1,1536]{2,1,0:T(1,128)S(1)}, u32[]{:S(2)}, u32[]{:S(2)}) %collective-permute-start.5) | collective-permute-done | bytes 49184 | tf_op jit(solution)/shard_map/ppermute | solution.py:22
  64.5 4.8 %collective-permute-start.8 = (f32[8,1,1536]{2,1,0:T(1,128)S(1)}, f32[8,1,1536]{2,1,0:T(1,128)S(1)}, u32[]{:S(2)}, u32[]{:S(2)}) collective-permute-start(f32[8,1,1536]{2,1,0:T(1,128)S(1)} %get-tuple-element.74), channel_id=1, source_target_pairs={{0,2},{2,4},{4,6},{6,8},{8,10},{10,12},{12,14},{1,3},{3,5},{5,7},{... | collective-permute-start | bytes 147464 | tf_op jit(solution)/shard_map/ppermute | solution.py:19
  71.1 4.3 %collective-permute-done.9 = f32[8,1,1536]{2,1,0:T(1,128)S(1)} collective-permute-done((f32[8,1,1536]{2,1,0:T(1,128)S(1)}, f32[8,1,1536]{2,1,0:T(1,128)S(1)}, u32[]{:S(2)}, u32[]{:S(2)}) %collective-permute-start.9) | collective-permute-done | bytes 49184 | tf_op jit(solution)/shard_map/ppermute | solution.py:22
  84.8 4.3 %collective-permute-done.13 = f32[8,1,1536]{2,1,0:T(1,128)S(1)} collective-permute-done((f32[8,1,1536]{2,1,0:T(1,128)S(1)}, f32[8,1,1536]{2,1,0:T(1,128)S(1)}, u32[]{:S(2)}, u32[]{:S(2)}) %collective-permute-start.13) | collective-permute-done | bytes 49184 | tf_op jit(solution)/shard_map/ppermute | solution.py:22
  94.0 3.6 all-to-all-start.1
  97.6 12.7 %all_gather.3 = f32[8,16,1536]{2,1,0:T(8,128)S(1)} all-gather(f32[8,8,1536]{2,1,0:T(8,128)S(1)} %fusion.38), channel_id=1, replica_groups=mesh['member'=2,'tile'=4,'tm'=2,'level'=2] {'tm'}, dimensions={1}, use_global_device_ids=true | all-gather | bytes 1179648 | tf_op jit(solution)/shard_map/all_gather | solution.py:71
  110.3 6.6 %copy.31 = f32[8,16,1536]{0,2,1:T(8,128)} copy(f32[8,16,1536]{2,1,0:T(8,128)S(1)} %all_gather.3) | data formatting | bytes 1572864 | tf_op jit(solution)/shard_map/all_gather | solution.py:71
  116.9 10.0 %gather_fusion.1 = f32[2048,8]{1,0:T(8,128)S(1)} fusion(f32[8,24576]{0,1:T(8,128)} %bitcast.53, s32[2048]{0:T(1024)S(1)} %broadcast_clamp_fusion.2), kind=kCustom, calls=%fused_computation.1 | custom fusion | bytes 139264 | tf_op jit(solution)/shard_map/gather | solution.py:79
  127.3 10.0 %gather_fusion.2 = f32[2048,8]{1,0:T(8,128)S(1)} fusion(f32[8,24576]{0,1:T(8,128)} %bitcast.54, s32[2048]{0:T(1024)S(1)} %broadcast_clamp_fusion.1), kind=kCustom, calls=%fused_computation.2 | custom fusion | bytes 139264 | tf_op jit(solution)/shard_map/gather | solution.py:79
  137.6 10.0 %gather_fusion.3 = f32[2048,8]{1,0:T(8,128)S(1)} fusion(f32[8,24576]{0,1:T(8,128)} %bitcast.55, s32[2048]{0:T(1024)S(1)} %broadcast_clamp_fusion), kind=kCustom, calls=%fused_computation.3 | custom fusion | bytes 139264 | tf_op jit(solution)/shard_map/gather | solution.py:79
  147.9 10.0 %gather_fusion = f32[2048,8]{1,0:T(8,128)S(1)} fusion(f32[8,24576]{0,1:T(8,128)} %bitcast.56, s32[2048]{0:T(1024)S(1)} %broadcast_clamp_fusion.3), kind=kCustom, calls=%fused_computation | custom fusion | bytes 139264 | tf_op jit(solution)/shard_map/gather | solution.py:79
  158.3 4.8 %all-to-all-start.4 = ((f32[4,4,128]{2,1,0:T(4,128)}), f32[4,4,128]{2,1,0:T(4,128)S(1)}, u32[]{:S(2)}, u32[]{:S(2)}) async-start(f32[4,4,128]{2,1,0:T(4,128)} %param.21), calls=%async_computation.4 | async-start | bytes 16384 | tf_op jit(solution)/shard_map/all_to_all | solution.py:63
  172.7 17.2 %scatter_custom_fusion = f32[8,24576]{0,1:T(8,128)} fusion(s32[2048]{0:T(1024)} %bitcast.87, f32[2048,8]{1,0:T(8,128)} %copy.36, f32[]{:T(128)} %constant.13.clone.1), kind=kCustom, calls=%fused_computation.8 | custom fusion | flops 16384 | bytes 786944 | tf_op jit(solution)/shard_map/scatter-add | solution.py:89
  189.8 19.6 %scatter_fusion = f32[8,24576]{0,1:T(8,128)} fusion(f32[8,24576]{0,1:T(8,128)} %scatter_custom_fusion, s32[2048]{0:T(1024)} %bitcast.77, f32[2048,8]{1,0:T(8,128)S(1)} %copy.37), kind=kCustom, calls=%fused_computation.5 | custom fusion | flops 16384 | bytes 204800 | tf_op jit(solution)/shard_map/scatter-add | solution.py:89
  209.4 19.5 %scatter_fusion.1 = f32[8,24576]{0,1:T(8,128)} fusion(f32[8,24576]{0,1:T(8,128)} %scatter_fusion, s32[2048]{0:T(1024)S(1)} %bitcast.76, f32[2048,8]{1,0:T(8,128)S(1)} %copy.38), kind=kCustom, calls=%fused_computation.6 | custom fusion | flops 16384 | bytes 204800 | tf_op jit(solution)/shard_map/scatter-add | solution.py:89
  228.9 19.5 %scatter_fusion.2 = f32[8,24576]{0,1:T(8,128)} fusion(f32[8,24576]{0,1:T(8,128)} %scatter_fusion.1, s32[2048]{0:T(1024)S(1)} %bitcast.75, f32[2048,8]{1,0:T(8,128)S(1)} %copy.39), kind=kCustom, calls=%fused_computation.7 | custom fusion | flops 16384 | bytes 204800 | tf_op jit(solution)/shard_map/scatter-add | solution.py:89
  248.3 8.3 %copy.40 = f32[8,16,1536]{2,1,0:T(8,128)} copy(f32[8,16,1536]{0,2,1:T(8,128)} %bitcast.52) | data formatting | bytes 1572864 | tf_op jit(solution)/shard_map/reshape | solution.py:91
  256.7 16.3 %reduce-scatter.2.cloned.1.call-done = f32[8,8,1536]{2,1,0:T(8,128)} async-done(((f32[8,16,1536]{2,1,0:T(8,128)}), f32[8,8,1536]{2,1,0:T(8,128)}) %reduce-scatter.2.cloned.1.call-update) | async-done | bytes 393232 | tf_op jit(solution)/shard_map/reduce_scatter | solution.py:90
  278.1 4.9 %collective-permute-done.17 = f32[8,1,1536]{2,1,0:T(1,128)S(1)} collective-permute-done((f32[8,1,1536]{2,1,0:T(1,128)S(1)}, f32[8,1,1536]{2,1,0:T(1,128)S(1)}, u32[]{:S(2)}, u32[]{:S(2)}) %collective-permute-start.17) | collective-permute-done | bytes 49184 | tf_op jit(solution)/shard_map/ppermute | solution.py:22
  287.9 4.8 %collective-permute-start.20 = (f32[8,1,1536]{2,1,0:T(1,128)S(1)}, f32[8,1,1536]{2,1,0:T(1,128)S(1)}, u32[]{:S(2)}, u32[]{:S(2)}) collective-permute-start(f32[8,1,1536]{2,1,0:T(1,128)S(1)} %get-tuple-element.56), channel_id=1, source_target_pairs={{0,2},{2,4},{4,6},{6,8},{8,10},{10,12},{12,14},{1,3},{3,5},{5,7},{... | collective-permute-start | bytes 147464 | tf_op jit(solution)/shard_map/ppermute | solution.py:19
  294.5 4.3 %collective-permute-done.21 = f32[8,1,1536]{2,1,0:T(1,128)S(1)} collective-permute-done((f32[8,1,1536]{2,1,0:T(1,128)S(1)}, f32[8,1,1536]{2,1,0:T(1,128)S(1)}, u32[]{:S(2)}, u32[]{:S(2)}) %collective-permute-start.21) | collective-permute-done | bytes 49184 | tf_op jit(solution)/shard_map/ppermute | solution.py:22
  308.2 4.3 %collective-permute-done.25 = f32[8,1,1536]{2,1,0:T(1,128)S(1)} collective-permute-done((f32[8,1,1536]{2,1,0:T(1,128)S(1)}, f32[8,1,1536]{2,1,0:T(1,128)S(1)}, u32[]{:S(2)}, u32[]{:S(2)}) %collective-permute-start.25) | collective-permute-done | bytes 49184 | tf_op jit(solution)/shard_map/ppermute | solution.py:22
  317.5 4.8 %collective-permute-start.28 = (f32[8,1,1536]{2,1,0:T(1,128)S(1)}, f32[8,1,1536]{2,1,0:T(1,128)S(1)}, u32[]{:S(2)}, u32[]{:S(2)}) collective-permute-start(f32[8,1,1536]{2,1,0:T(1,128)S(1)} %get-tuple-element.44), channel_id=1, source_target_pairs={{0,2},{2,4},{4,6},{6,8},{8,10},{10,12},{12,14},{1,3},{3,5},{5,7},{... | collective-permute-start | bytes 147464 | tf_op jit(solution)/shard_map/ppermute | solution.py:19
  324.0 4.3 %collective-permute-done.29 = f32[8,1,1536]{2,1,0:T(1,128)S(1)} collective-permute-done((f32[8,1,1536]{2,1,0:T(1,128)S(1)}, f32[8,1,1536]{2,1,0:T(1,128)S(1)}, u32[]{:S(2)}, u32[]{:S(2)}) %collective-permute-start.29) | collective-permute-done | bytes 49184 | tf_op jit(solution)/shard_map/ppermute | solution.py:22
  333.9 30.3 %all-reduce = (f32[]{:T(128)}, f32[]{:T(128)}, f32[]{:T(128)}, f32[]{:T(128)}) all-reduce(f32[]{:T(128)} %get-tuple-element.5, f32[]{:T(128)} %get-tuple-element.6, f32[]{:T(128)} %get-tuple-element.4, f32[]{:T(128)} %get-tuple-element.3), channel_id=1, replica_groups=mesh['member'=2,'tile'=4,'tm'=2,'level'=2] {'tile','tm','level'}, use_global_device_ids=true, to_apply=%region_1.2 | all-reduce | flops 4 | bytes 32 | tf_op jit(solution)/shard_map/psum | solution.py:94
  (135 shorter events, 84.2 us)
Async XLA Ops:
  8.4 30.8 %collective-permute-start = (f32[8,1,1536]{2,1,0:T(1,128)S(1)}, f32[8,1,1536]{2,1,0:T(1,128)S(1)}, u32[]{:S(2)}, u32[]{:S(2)}) collective-permute-start(f32[8,1,1536]{2,1,0:T(1,128)S(1)} %get-tuple-element.86), channel_id=1, source_target_pairs={{0,2},{2,4},{4,6},{6,8},{8,10},{10,12},{12,14},{1,3},{3,5},{5,7},{... | collective-permute-start | bytes 147464 | tf_op jit(solution)/shard_map/ppermute | solution.py:19
  13.3 25.9 %collective-permute-start.1 = (f32[8,1,1536]{2,1,0:T(1,128)S(1)}, f32[8,1,1536]{2,1,0:T(1,128)S(1)}, u32[]{:S(2)}, u32[]{:S(2)}) collective-permute-start(f32[8,1,1536]{2,1,0:T(1,128)S(1)} %get-tuple-element.87), channel_id=1, source_target_pairs={{2,0},{4,2},{6,4},{8,6},{10,8},{12,10},{14,12},{3,1},{5,3},{7,5},{... | collective-permute-start | bytes 147464 | tf_op jit(solution)/shard_map/ppermute | solution.py:22
  14.6 12.5 %all-to-all-start = ((s32[4,4,128]{2,1,0:T(4,128)}), s32[4,4,128]{2,1,0:T(4,128)S(1)}, u32[]{:S(2)}, u32[]{:S(2)}) async-start(s32[4,4,128]{2,1,0:T(4,128)} %param.16), calls=%async_computation | async-start | bytes 16384 | tf_op jit(solution)/shard_map/all_to_all | solution.py:66
  27.1 8.8 %all-to-all-start.2 = ((s32[4,4,128]{2,1,0:T(4,128)}), s32[4,4,128]{2,1,0:T(4,128)S(1)}, u32[]{:S(2)}, u32[]{:S(2)}) async-start(s32[4,4,128]{2,1,0:T(4,128)} %param.17), calls=%async_computation.2 | async-start | bytes 16384 | tf_op jit(solution)/shard_map/all_to_all | solution.py:67
  35.9 8.9 %all-to-all-start.5 = ((f32[4,4,4,128]{3,2,1,0:T(4,128)}), f32[4,4,4,128]{3,2,1,0:T(4,128)S(1)}, u32[]{:S(2)}, u32[]{:S(2)}) async-start(f32[4,4,4,128]{3,2,1,0:T(4,128)} %param.19), calls=%async_computation.5 | async-start | bytes 65536 | tf_op jit(solution)/shard_map/all_to_all | solution.py:61
  40.1 8.0 %collective-permute-start.2 = (f32[1,10,1536]{2,1,0:T(8,128)S(1)}, f32[1,10,1536]{2,1,0:T(8,128)S(1)}, u32[]{:S(2)}, u32[]{:S(2)}) collective-permute-start(f32[1,10,1536]{2,1,0:T(8,128)S(1)} %get-tuple-element.37), channel_id=1, source_target_pairs={{0,1},{2,3},{4,5},{6,7},{8,9},{10,11},{12,13},{14,15},{16,17},{18,... | collective-permute-start | bytes 184328 | tf_op jit(solution)/shard_map/ppermute | solution.py:19
  41.4 6.7 %collective-permute-start.3 = (f32[1,10,1536]{2,1,0:T(8,128)S(1)}, f32[1,10,1536]{2,1,0:T(8,128)S(1)}, u32[]{:S(2)}, u32[]{:S(2)}) collective-permute-start(f32[1,10,1536]{2,1,0:T(8,128)S(1)} %get-tuple-element.38), channel_id=1, source_target_pairs={{1,0},{3,2},{5,4},{7,6},{9,8},{11,10},{13,12},{15,14},{17,16},{19,... | collective-permute-start | bytes 184328 | tf_op jit(solution)/shard_map/ppermute | solution.py:22
  44.8 49.2 %all-to-all-start.3 = ((s32[4,1,4]{2,1,0:T(1,128)}), s32[4,1,4]{2,1,0:T(1,128)S(1)}, u32[]{:S(2)}, u32[]{:S(2)}) async-start(s32[4,1,4]{2,1,0:T(1,128)} %bitcast.89), calls=%async_computation.3 | async-start | bytes 4096 | tf_op jit(solution)/shard_map/all_to_all | solution.py:68
  50.2 4.2 %collective-permute-start.4 = (f32[8,1,1536]{2,1,0:T(1,128)S(1)}, f32[8,1,1536]{2,1,0:T(1,128)S(1)}, u32[]{:S(2)}, u32[]{:S(2)}) collective-permute-start(f32[8,1,1536]{2,1,0:T(1,128)S(1)} %get-tuple-element.80), channel_id=1, source_target_pairs={{0,2},{2,4},{4,6},{6,8},{8,10},{10,12},{12,14},{1,3},{3,5},{5,7},{... | collective-permute-start | bytes 147464 | tf_op jit(solution)/shard_map/ppermute | solution.py:19
  52.7 6.8 %collective-permute-start.5 = (f32[8,1,1536]{2,1,0:T(1,128)S(1)}, f32[8,1,1536]{2,1,0:T(1,128)S(1)}, u32[]{:S(2)}, u32[]{:S(2)}) collective-permute-start(f32[8,1,1536]{2,1,0:T(1,128)S(1)} %get-tuple-element.81), channel_id=1, source_target_pairs={{2,0},{4,2},{6,4},{8,6},{10,8},{12,10},{14,12},{3,1},{5,3},{7,5},{... | collective-permute-start | bytes 147464 | tf_op jit(solution)/shard_map/ppermute | solution.py:22
  60.9 3.2 collective-permute-start.7
  64.5 6.6 %collective-permute-start.8 = (f32[8,1,1536]{2,1,0:T(1,128)S(1)}, f32[8,1,1536]{2,1,0:T(1,128)S(1)}, u32[]{:S(2)}, u32[]{:S(2)}) collective-permute-start(f32[8,1,1536]{2,1,0:T(1,128)S(1)} %get-tuple-element.74), channel_id=1, source_target_pairs={{0,2},{2,4},{4,6},{6,8},{8,10},{10,12},{12,14},{1,3},{3,5},{5,7},{... | collective-permute-start | bytes 147464 | tf_op jit(solution)/shard_map/ppermute | solution.py:19
  69.3 6.0 %collective-permute-start.9 = (f32[8,1,1536]{2,1,0:T(1,128)S(1)}, f32[8,1,1536]{2,1,0:T(1,128)S(1)}, u32[]{:S(2)}, u32[]{:S(2)}) collective-permute-start(f32[8,1,1536]{2,1,0:T(1,128)S(1)} %get-tuple-element.75), channel_id=1, source_target_pairs={{2,0},{4,2},{6,4},{8,6},{10,8},{12,10},{14,12},{3,1},{5,3},{7,5},{... | collective-permute-start | bytes 147464 | tf_op jit(solution)/shard_map/ppermute | solution.py:22
  76.7 3.2 collective-permute-start.11
  80.3 4.6 %collective-permute-start.12 = (f32[8,1,1536]{2,1,0:T(1,128)S(1)}, f32[8,1,1536]{2,1,0:T(1,128)S(1)}, u32[]{:S(2)}, u32[]{:S(2)}) collective-permute-start(f32[8,1,1536]{2,1,0:T(1,128)S(1)} %get-tuple-element.68), channel_id=1, source_target_pairs={{0,2},{2,4},{4,6},{6,8},{8,10},{10,12},{12,14},{1,3},{3,5},{5,7},{... | collective-permute-start | bytes 147464 | tf_op jit(solution)/shard_map/ppermute | solution.py:19
  83.1 6.0 %collective-permute-start.13 = (f32[8,1,1536]{2,1,0:T(1,128)S(1)}, f32[8,1,1536]{2,1,0:T(1,128)S(1)}, u32[]{:S(2)}, u32[]{:S(2)}) collective-permute-start(f32[8,1,1536]{2,1,0:T(1,128)S(1)} %get-tuple-element.69), channel_id=1, source_target_pairs={{2,0},{4,2},{6,4},{8,6},{10,8},{12,10},{14,12},{3,1},{5,3},{7,5},{... | collective-permute-start | bytes 147464 | tf_op jit(solution)/shard_map/ppermute | solution.py:22
  90.4 3.2 collective-permute-start.15
  94.0 64.3 %all-to-all-start.1 = ((f32[4,4,8,128]{3,2,1,0:T(8,128)}), f32[4,4,8,128]{3,2,1,0:T(8,128)S(1)}, u32[]{:S(2)}, u32[]{:S(2)}) async-start(f32[4,4,8,128]{3,2,1,0:T(8,128)} %param.20), calls=%async_computation.1 | async-start | bytes 131072 | tf_op jit(solution)/shard_map/all_to_all | solution.py:62
  158.3 10.4 %all-to-all-start.4 = ((f32[4,4,128]{2,1,0:T(4,128)}), f32[4,4,128]{2,1,0:T(4,128)S(1)}, u32[]{:S(2)}, u32[]{:S(2)}) async-start(f32[4,4,128]{2,1,0:T(4,128)} %param.21), calls=%async_computation.4 | async-start | bytes 16384 | tf_op jit(solution)/shard_map/all_to_all | solution.py:63
  163.1 109.9 %reduce-scatter.2.cloned.1.call-start = ((), (), s32[]{:S(2)}) async-start(), calls=%async_computation.7 | async-start | bytes 1179648 | tf_op jit(solution)/shard_map/reduce_scatter | solution.py:90
  274.1 4.0 %collective-permute-start.16 = (f32[8,1,1536]{2,1,0:T(1,128)S(1)}, f32[8,1,1536]{2,1,0:T(1,128)S(1)}, u32[]{:S(2)}, u32[]{:S(2)}) collective-permute-start(f32[8,1,1536]{2,1,0:T(1,128)S(1)} %get-tuple-element.62), channel_id=1, source_target_pairs={{0,2},{2,4},{4,6},{6,8},{8,10},{10,12},{12,14},{1,3},{3,5},{5,7},{... | collective-permute-start | bytes 147464 | tf_op jit(solution)/shard_map/ppermute | solution.py:19
  276.4 6.6 %collective-permute-start.17 = (f32[8,1,1536]{2,1,0:T(1,128)S(1)}, f32[8,1,1536]{2,1,0:T(1,128)S(1)}, u32[]{:S(2)}, u32[]{:S(2)}) collective-permute-start(f32[8,1,1536]{2,1,0:T(1,128)S(1)} %get-tuple-element.63), channel_id=1, source_target_pairs={{2,0},{4,2},{6,4},{8,6},{10,8},{12,10},{14,12},{3,1},{5,3},{7,5},{... | collective-permute-start | bytes 147464 | tf_op jit(solution)/shard_map/ppermute | solution.py:22
  284.3 3.2 collective-permute-start.19
  287.9 6.6 %collective-permute-start.20 = (f32[8,1,1536]{2,1,0:T(1,128)S(1)}, f32[8,1,1536]{2,1,0:T(1,128)S(1)}, u32[]{:S(2)}, u32[]{:S(2)}) collective-permute-start(f32[8,1,1536]{2,1,0:T(1,128)S(1)} %get-tuple-element.56), channel_id=1, source_target_pairs={{0,2},{2,4},{4,6},{6,8},{8,10},{10,12},{12,14},{1,3},{3,5},{5,7},{... | collective-permute-start | bytes 147464 | tf_op jit(solution)/shard_map/ppermute | solution.py:19
  292.7 6.0 %collective-permute-start.21 = (f32[8,1,1536]{2,1,0:T(1,128)S(1)}, f32[8,1,1536]{2,1,0:T(1,128)S(1)}, u32[]{:S(2)}, u32[]{:S(2)}) collective-permute-start(f32[8,1,1536]{2,1,0:T(1,128)S(1)} %get-tuple-element.57), channel_id=1, source_target_pairs={{2,0},{4,2},{6,4},{8,6},{10,8},{12,10},{14,12},{3,1},{5,3},{7,5},{... | collective-permute-start | bytes 147464 | tf_op jit(solution)/shard_map/ppermute | solution.py:22
  300.1 3.2 collective-permute-start.23
  303.7 4.6 %collective-permute-start.24 = (f32[8,1,1536]{2,1,0:T(1,128)S(1)}, f32[8,1,1536]{2,1,0:T(1,128)S(1)}, u32[]{:S(2)}, u32[]{:S(2)}) collective-permute-start(f32[8,1,1536]{2,1,0:T(1,128)S(1)} %get-tuple-element.50), channel_id=1, source_target_pairs={{0,2},{2,4},{4,6},{6,8},{8,10},{10,12},{12,14},{1,3},{3,5},{5,7},{... | collective-permute-start | bytes 147464 | tf_op jit(solution)/shard_map/ppermute | solution.py:19
  306.5 6.0 %collective-permute-start.25 = (f32[8,1,1536]{2,1,0:T(1,128)S(1)}, f32[8,1,1536]{2,1,0:T(1,128)S(1)}, u32[]{:S(2)}, u32[]{:S(2)}) collective-permute-start(f32[8,1,1536]{2,1,0:T(1,128)S(1)} %get-tuple-element.51), channel_id=1, source_target_pairs={{2,0},{4,2},{6,4},{8,6},{10,8},{12,10},{14,12},{3,1},{5,3},{7,5},{... | collective-permute-start | bytes 147464 | tf_op jit(solution)/shard_map/ppermute | solution.py:22
  313.8 3.2 collective-permute-start.27
  317.5 6.6 %collective-permute-start.28 = (f32[8,1,1536]{2,1,0:T(1,128)S(1)}, f32[8,1,1536]{2,1,0:T(1,128)S(1)}, u32[]{:S(2)}, u32[]{:S(2)}) collective-permute-start(f32[8,1,1536]{2,1,0:T(1,128)S(1)} %get-tuple-element.44), channel_id=1, source_target_pairs={{0,2},{2,4},{4,6},{6,8},{8,10},{10,12},{12,14},{1,3},{3,5},{5,7},{... | collective-permute-start | bytes 147464 | tf_op jit(solution)/shard_map/ppermute | solution.py:19
  322.3 6.0 %collective-permute-start.29 = (f32[8,1,1536]{2,1,0:T(1,128)S(1)}, f32[8,1,1536]{2,1,0:T(1,128)S(1)}, u32[]{:S(2)}, u32[]{:S(2)}) collective-permute-start(f32[8,1,1536]{2,1,0:T(1,128)S(1)} %get-tuple-element.45), channel_id=1, source_target_pairs={{2,0},{4,2},{6,4},{8,6},{10,8},{12,10},{14,12},{3,1},{5,3},{7,5},{... | collective-permute-start | bytes 147464 | tf_op jit(solution)/shard_map/ppermute | solution.py:22
  329.6 3.2 collective-permute-start.31
  (12 other events, 464.3 us)
Sparse Core Ops, SparseCore 0:
  256.8 16.1 reduce-scatter.1
where the time goes:
time: 378 us; the launch traced here: 376 us
  other arithmetic  86.4 us (23%)
  starting transfers between devices  85.8 us (23%)
  waiting for transfers between devices  74.9 us (20%)
  local copies, waits for them, and re-layouts  65 us (17%)
  blocking collectives  45.5 us (12%)
  between operations  18.6 us (5%)
    scatter-add x4, other arithmetic, local(): tile_adjoint = tile_adjoint.at[:, cells[k].reshape(-1)].add(values)  75.7 us
    ppermute x16, waiting for transfers between devices, padded_2(): lax.ppermute(lax.slice_in_dim(block, 0, width, axis=dim), axis, backward)  43.9 us
    gather x8, local copies, waits for them, and re-layouts, local(): inner = inner + weights_h[:, :, k, :][None] * flat[:, cells[k]]  41.3 us
    ppermute x16, starting transfers between devices, padded_2(): lax.ppermute(lax.slice_in_dim(block, block.shape[dim] - width, None, axis...  40 us
    psum x1, blocking collectives, local(): lax.psum((jnp.sum(residual * residual), jnp.sum(direction * image), jnp.s...  30.3 us
    ppermute x16, starting transfers between devices, padded_2(): lax.ppermute(lax.slice_in_dim(block, 0, width, axis=dim), axis, backward)  20.7 us
    reduce_scatter x1, waiting for transfers between devices, local(): lax.psum_scatter(tile_adjoint.reshape(tile_field.shape), 'tm', scatter_di...  16.3 us
    all_gather x1, blocking collectives, local(): tile_field = lax.all_gather(increment, 'tm', axis=1, tiled=True)  12.7 us
  transfers between devices with their start and end apart: 39, of which 26 were waited for; matrix products, arithmetic and copies ran while one was open for 15% of the time, Pallas kernels for 0%

commit v1 on v0

v1 whole, which is shorter than its diff:
```python
import functools

import jax
import jax.numpy as jnp
from jax import lax
from jax.experimental import pallas as pl
from jax.experimental.pallas import tpu as pltpu
from jax.sharding import PartitionSpec as P

K_DIFF = 4
HALO = K_DIFF
center_coef = 0.1
row_coef = 0.2
level_coef = 0.05
MESH = pl.DeviceIdType.MESH
f32 = jnp.float32
bf16 = jnp.bfloat16


def split(x):
    high = x.astype(bf16)
    return high, (x - high.astype(f32)).astype(bf16)


def kernel(
    sizes,
    residual, direction, sigma, decay, cell, slot, count, horiz, vert, prec,
    image, scal,
    a0, a1, t0, t1, top, bot, rd, ru, xd, xu, xc, pack, obs, fields, parts, models,
    acc, ip1, ip2,
    halo_send, halo_recv, obs_send, obs_recv, mod_send, mod_recv,
    s1_send, s1_recv, s2_send, s2_recv,
):
    nt, ntm, nlev = sizes
    levels, rows, width = direction.shape
    blocks = cell.shape[1]
    ng, ngroup = nt * ntm, ntm * nlev
    member = lax.axis_index("member")
    tile = lax.axis_index("tile")
    tm = lax.axis_index("tm")
    lev = lax.axis_index("level")
    g = tile * ntm + tm
    other = 1 - lev
    has_up, has_down = g > 0, g < ng - 1

    def dev(index, level):
        return (member, index // ntm, lax.rem(index, ntm), level)

    barrier = pltpu.get_barrier_semaphore()
    everyone = ng * nlev
    me = g * nlev + lev
    for i in range(1, everyone):
        to = lax.rem(me + i, everyone)
        pl.semaphore_signal(
            barrier, inc=1, device_id=dev(to // nlev, lax.rem(to, nlev)), device_id_type=MESH
        )

    sub = lax.broadcasted_iota(jnp.int32, (rows, width), 0)
    low_half = sub < HALO

    def pack_rows(source, base):
        for j in range(levels // 2):
            even, odd = source[base + 2 * j], pltpu.roll(source[base + 2 * j + 1], HALO, 0)
            top[j] = jnp.where(low_half, even, odd)
            bot[j] = jnp.where(low_half, odd, even)

    def halo_copies(phase, source, base):
        up, down = g - 1, g + 1
        half = pl.ds(2 * other, 2)
        edge = pl.ds(base + HALO * other, HALO)
        plan = [
            (top, rd.at[phase], up, lev, has_up, has_down),
            (bot, ru.at[phase], down, lev, has_down, has_up),
            (top.at[half], xd.at[phase], up, other, has_up, has_down),
            (bot.at[half], xu.at[phase], down, other, has_down, has_up),
            (source.at[edge], xc.at[phase], g, other, None, None),
        ]
        return [
            (
                pltpu.make_async_remote_copy(
                    src_ref=src, dst_ref=dst,
                    send_sem=halo_send.at[phase, n], recv_sem=halo_recv.at[phase, n],
                    device_id=dev(jnp.clip(to, 0, ng - 1), level), device_id_type=MESH,
                ),
                sends, gets,
            )
            for n, (src, dst, to, level, sends, gets) in enumerate(plan)
        ]

    def when(condition, action):
        if condition is None:
            action()
        else:
            pl.when(condition)(action)

    pack_rows(direction, 0)
    pl.semaphore_wait(barrier, everyone - 1)
    halo1 = halo_copies(0, direction, 0)
    for copy, sends, gets in halo1:
        when(sends, copy.start)

    eff_rows = blocks * levels
    h_rows = eff_rows + blocks * 4
    level_id = lax.broadcasted_iota(jnp.int32, (levels, 128), 0)
    lane = lax.broadcasted_iota(jnp.int32, (1, 128), 1)
    rate = jnp.zeros((levels, 128), f32)
    for l in range(levels):
        rate = jnp.where(level_id == l, decay[l], rate)

    def pack_tile(t, carry):
        for b in range(blocks):
            s = slot[t, b : b + 1, :].astype(f32)
            pack[t, b * levels : (b + 1) * levels, :] = vert[t, b] * jnp.exp(-s * rate)
            pack[t, eff_rows + 4 * b : eff_rows + 4 * b + 4, :] = horiz[t, b]
            pack[t, h_rows + b : h_rows + b + 1, :] = jnp.where(
                lane < count[t, b], prec[t, b : b + 1, :], 0.0
            )
        pack[t, h_rows + blocks : h_rows + 2 * blocks, :] = cell[t].astype(f32)
        return carry

    lax.fori_loop(0, nt, pack_tile, 0)

    def obs_copy(i):
        to = lax.rem(g + i, ng)
        return pltpu.make_async_remote_copy(
            src_ref=pack.at[to // ntm], dst_ref=obs.at[g],
            send_sem=obs_send.at[i], recv_sem=obs_recv.at[i],
            device_id=dev(to, lev), device_id_type=MESH,
        )

    def obs_arrival(i):
        return pltpu.make_async_remote_copy(
            src_ref=pack.at[tile], dst_ref=obs.at[lax.rem(g - i + ng, ng)],
            send_sem=obs_send.at[i], recv_sem=obs_recv.at[i],
            device_id=dev(lax.rem(g + i, ng), lev), device_id_type=MESH,
        )

    for i in range(1, ng):
        obs_copy(i).start()
    obs[g] = pack[tile]

    inside = (low_half & has_down) | (jnp.logical_not(low_half) & has_up)

    def unpack(down, up, n, base):
        for j in range(n):
            a1[base + 2 * j] = jnp.where(inside, jnp.where(low_half, down[j], up[j]), 0.0)
            a1[base + 2 * j + 1] = jnp.where(
                inside, pltpu.roll(jnp.where(low_half, up[j], down[j]), HALO, 0), 0.0
            )

    zero = jnp.zeros((rows, width), f32)
    for buffer in (a0, a1, t0, t1):
        buffer[0] = zero
        buffer[levels + HALO + 1] = zero
    own = 1 + HALO * lev
    far = 1 + levels * other

    def receive(phase, copies):
        for copy, sends, gets in copies:
            when(gets, copy.wait_recv)
        unpack(rd.at[phase], ru.at[phase], levels // 2, own)
        unpack(xd.at[phase], xu.at[phase], HALO // 2, far)
        for l in range(HALO):
            a0[far + l] = xc[phase, l]
        for copy, sends, gets in copies:
            when(sends, copy.wait_send)

    def smooth_step(step, src0, src1, dst0, dst1):
        def body(i, carry):
            l = 1 + step * lev + i
            full = jnp.concatenate([src0[l], src1[l]], axis=0)
            near = (
                pltpu.roll(full, 1, 0) + pltpu.roll(full, 2 * rows - 1, 0)
                + pltpu.roll(full, 1, 1) + pltpu.roll(full, width - 1, 1)
            )
            main = center_coef * full + row_coef * near
            dst0[l] = main[:rows] + level_coef * (src0[l - 1] + src0[l + 1])
            if step < K_DIFF:
                side = main[rows:] + level_coef * (src1[l - 1] + src1[l + 1])
                dst1[l] = jnp.where(inside, side, 0.0)
            return carry

        lax.fori_loop(0, levels + HALO - step, body, 0)

    def smooth():
        smooth_step(1, a0, a1, t0, t1)
        smooth_step(2, t0, t1, a0, a1)
        smooth_step(3, a0, a1, t0, t1)
        smooth_step(4, t0, t1, a0, a1)

    a0[pl.ds(own, levels)] = direction[...]
    receive(0, halo1)
    smooth()

    cells_here = levels * rows
    increment = (sigma[...] * a0[pl.ds(own, levels)]).reshape(cells_here, width)
    high, low = split(increment)
    fields[0:cells_here] = high
    fields[2 * cells_here : 3 * cells_here] = low
    high, low = split(pltpu.roll(increment, width - 1, 1))
    fields[cells_here : 2 * cells_here] = high
    fields[3 * cells_here : 4 * cells_here] = low

    for i in range(1, ng):
        obs_arrival(i).wait_recv()

    nobs = blocks * 128
    row_id = lax.broadcasted_iota(jnp.int32, (rows, nobs), 0).astype(f32)
    first_row = (tm * rows).astype(f32)

    def lanes(q, start, stride):
        return jnp.concatenate(
            [obs[q, start + b * stride : start + b * stride + 1, :] for b in range(blocks)], axis=1
        )

    def stencil(q):
        c = lanes(q, h_rows + blocks, 1)
        row = jnp.floor((c + 0.5) * (1.0 / width))
        col = (c - row * width).astype(jnp.int32)
        row = row - first_row
        lower, upper = row_id == row, row_id == row + 1.0
        weights = [
            jnp.where(lower, lanes(q, eff_rows + k, 4), 0.0)
            + jnp.where(upper, lanes(q, eff_rows + 2 + k, 4), 0.0)
            for k in range(2)
        ]
        col_id = lax.broadcasted_iota(jnp.int32, (width, nobs), 0)
        onehot = jnp.where(col_id == col, 1.0, 0.0).astype(bf16)
        return weights, onehot

    def gather(q, carry):
        weights, onehot = stencil(q)
        values = jnp.dot(fields[...], onehot, preferred_element_type=f32)
        values = values[: 2 * cells_here] + values[2 * cells_here :]
        total = jnp.zeros((rows, nobs), f32)
        for k in range(2):
            part = jnp.zeros((rows, nobs), f32)
            for l in range(levels):
                at = k * cells_here + l * rows
                part = part + lanes(q, l, levels) * values[at : at + rows]
            total = total + part * weights[k]
        total = jnp.sum(total, axis=0, keepdims=True)
        parts[q] = jnp.concatenate(
            [total[:, 128 * b : 128 * (b + 1)] for b in range(blocks)]
            + [jnp.zeros((8 - blocks, 128), f32)],
            axis=0,
        )
        return carry

    lax.fori_loop(0, ng, gather, 0)

    tg = tm * nlev + lev

    def exchange(i, src, slots, send, recv):
        to = lax.rem(tg + i, ngroup)
        came = lax.rem(tg - i + ngroup, ngroup)
        where = (member, tile, to // nlev, lax.rem(to, nlev))
        return [
            pltpu.make_async_remote_copy(
                src_ref=src, dst_ref=slots.at[at], send_sem=send.at[i], recv_sem=recv.at[i],
                device_id=where, device_id_type=MESH,
            )
            for at in (tg, came)
        ]

    swaps = [exchange(i, parts, models, mod_send, mod_recv) for i in range(1, ngroup)]
    for out, _ in swaps:
        out.start()
    models[tg] = parts[...]
    acc[...] = jnp.zeros_like(acc)
    for _, back in swaps:
        back.wait_recv()

    def scatter(q, carry):
        weights, onehot = stencil(q)
        model = models[0, q]
        for k in range(1, ngroup):
            model = model + models[k, q]
        departure = jnp.concatenate([model[b : b + 1] for b in range(blocks)], axis=1)
        departure = departure * lanes(q, h_rows, 1)
        scaled = [lanes(q, l, levels) * departure for l in range(levels)]
        values = jnp.concatenate(
            [scaled[l] * weights[k] for k in range(2) for l in range(levels)], axis=0
        )
        acc[...] += lax.dot_general(
            jnp.concatenate(split(values), axis=0), onehot, (((1,), (1,)), ((), ())),
            preferred_element_type=f32,
        )
        return carry

    lax.fori_loop(0, ng, scatter, 0)
    adjoint = acc[: 2 * cells_here] + acc[2 * cells_here :]
    adjoint = adjoint[:cells_here] + pltpu.roll(adjoint[cells_here:], 1, 1)
    a0[pl.ds(own, levels)] = sigma[...] * adjoint.reshape(levels, rows, width)
    pack_rows(a0, own)
    halo2 = halo_copies(1, a0, own)
    for copy, sends, gets in halo2:
        when(sends, copy.start)
    receive(1, halo2)
    smooth()

    sums = [jnp.zeros((rows, width), f32)] * 4
    for l in range(levels):
        d, r = direction[l], residual[l]
        im = d + a0[own + l]
        image[l] = im
        for n, term in enumerate((r * r, d * im, r * im, im * im)):
            sums[n] = sums[n] + term
    lines = []
    for total in sums:
        total = jnp.sum(total, axis=0, keepdims=True)
        line = total[:, :128]
        for at in range(128, width, 128):
            line = line + total[:, at : at + 128]
        lines.append(line)
    ip1[tg] = jnp.concatenate(lines + [jnp.zeros((4, 128), f32)], axis=0)
    swaps1 = [exchange(i, ip1.at[tg], ip1, s1_send, s1_recv) for i in range(1, ngroup)]
    for out, _ in swaps1:
        out.start()
    for _, back in swaps1:
        back.wait_recv()
    total = ip1[0]
    for k in range(1, ngroup):
        total = total + ip1[k]
    ip2[tile] = total
    swaps2 = []
    for i in range(1, nt):
        swaps2.append(
            [
                pltpu.make_async_remote_copy(
                    src_ref=ip2.at[tile], dst_ref=ip2.at[at],
                    send_sem=s2_send.at[i], recv_sem=s2_recv.at[i],
                    device_id=(member, lax.rem(tile + i, nt), tm, lev), device_id_type=MESH,
                )
                for at in (tile, lax.rem(tile - i + nt, nt))
            ]
        )
    for out, _ in swaps2:
        out.start()
    for _, back in swaps2:
        back.wait_recv()
    total = ip2[0]
    for k in range(1, nt):
        total = total + ip2[k]
    total = jnp.broadcast_to(jnp.sum(total, axis=1, keepdims=True), (8, 128))
    norm_old, curvature, cross, image_norm = (total[n : n + 1] for n in range(4))
    alpha = norm_old / curvature
    norm_new = norm_old - 2.0 * alpha * cross + alpha * alpha * image_norm
    scal[...] = jnp.concatenate([alpha, norm_new / norm_old, jnp.zeros((6, 128), f32)], axis=0)

    for i in range(1, ng):
        obs_copy(i).wait_send()
    for out, _ in swaps + swaps1 + swaps2:
        out.wait_send()


def local(
    sizes,
    control,
    residual,
    direction,
    sigma,
    decay_rate,
    obs_cell,
    observation_slot,
    block_count,
    horiz_weight,
    vert_weight,
    obs_precision,
):
    nt, ntm, nlev = sizes
    levels, rows, width = direction.shape
    blocks = obs_cell.shape[1]
    ng, ngroup = nt * ntm, ntm * nlev
    packed = blocks * (levels + 6)
    vmem = pl.BlockSpec(memory_space=pltpu.VMEM)
    smem = pl.BlockSpec(memory_space=pltpu.SMEM)
    field = pltpu.VMEM((levels + HALO + 2, rows, width), f32)
    dma = pltpu.SemaphoreType.DMA
    image, scal = pl.pallas_call(
        functools.partial(kernel, sizes),
        out_shape=(
            jax.ShapeDtypeStruct((levels, rows, width), f32),
            jax.ShapeDtypeStruct((8, 128), f32),
        ),
        in_specs=[vmem, vmem, vmem, smem, vmem, vmem, smem, vmem, vmem, vmem],
        out_specs=(vmem, vmem),
        scratch_shapes=[
            field, field, field, field,
            pltpu.VMEM((levels // 2, rows, width), f32),
            pltpu.VMEM((levels // 2, rows, width), f32),
            pltpu.VMEM((2, levels // 2, rows, width), f32),
            pltpu.VMEM((2, levels // 2, rows, width), f32),
            pltpu.VMEM((2, HALO // 2, rows, width), f32),
            pltpu.VMEM((2, HALO // 2, rows, width), f32),
            pltpu.VMEM((2, HALO, rows, width), f32),
            pltpu.VMEM((nt, packed, 128), f32),
            pltpu.VMEM((ng, packed, 128), f32),
            pltpu.VMEM((4 * levels * rows, width), bf16),
            pltpu.VMEM((ng, 8, 128), f32),
            pltpu.VMEM((ngroup, ng, 8, 128), f32),
            pltpu.VMEM((4 * levels * rows, width), f32),
            pltpu.VMEM((ngroup, 8, 128), f32),
            pltpu.VMEM((nt, 8, 128), f32),
            dma((2, 5)), dma((2, 5)),
            dma((ng,)), dma((ng,)),
            dma((ngroup,)), dma((ngroup,)),
            dma((ngroup,)), dma((ngroup,)),
            dma((nt,)), dma((nt,)),
        ],
        compiler_params=pltpu.CompilerParams(
            collective_id=0, has_side_effects=True, vmem_limit_bytes=48 * 1024 * 1024
        ),
    )(
        residual, direction, sigma, decay_rate, obs_cell, observation_slot, block_count,
        horiz_weight, vert_weight, obs_precision,
    )
    alpha, beta = scal[0, 0], scal[1, 0]
    residual_new = residual - alpha * image
    control_new = control + alpha * direction
    updated_direction = residual_new + beta * direction
    return (control_new, residual_new, updated_direction)


def solution(mesh):
    grid = P(("member", "level"), ("tile", "tm"), None)
    placed = (
        grid,
        grid,
        grid,
        grid,
        P(("member", "level")),
        P(("member", "tile"), "tm", None),
        P(("member", "tile"), "tm", None),
        P(("member", "tile"), "tm"),
        P(("member", "tile"), "tm", None, None),
        P(("member", "tile"), "tm", "level", None),
        P(("member", "tile"), "tm", None),
    )
    sizes = tuple(mesh.shape[axis] for axis in ("tile", "tm", "level"))
    return jax.shard_map(
        functools.partial(local, sizes),
        mesh=mesh,
        in_specs=placed,
        out_specs=(grid, grid, grid),
        check_vma=False,
    )
```

time: 378 us -> 78 us (0.21)
  starting transfers between devices: 85.8 us -> 0 us
  other arithmetic: 86.4 us -> 2.27 us
  waiting for transfers between devices: 74.9 us -> 0 us
  Pallas kernels: 0 us -> 65.9 us
  local copies, waits for them, and re-layouts: 65 us -> 8.55 us
  blocking collectives: 45.5 us -> 0 us
  between operations: 18.6 us -> 0.66 us
    scatter-add x4 -> x0, other arithmetic: 75.7 us -> none  [local(): tile_adjoint = tile_adjoint.at[:, cells[k].reshape(-1)].add(values)]
    pallas_call x0 -> x1, Pallas kernels: none -> 65.9 us  [local(): pl.pallas_call(functools.partial(kernel, sizes), out_shape=(jax.ShapeDtyp...]
    ppermute x32 -> x0, starting transfers between devices: 60.7 us -> none  [the longest x16 40 us: padded_2(): lax.ppermute(lax.slice_in_dim(block, block.shape[dim] - width, None, axis...]
    ppermute x32 -> x0, waiting for transfers between devices: 45.8 us -> none  [the longest x16 43.9 us: padded_2(): lax.ppermute(lax.slice_in_dim(block, 0, width, axis=dim), axis, backward)]
    gather x8 -> x0, local copies, waits for them, and re-layouts: 41.3 us -> none  [local(): inner = inner + weights_h[:, :, k, :][None] * flat[:, cells[k]]]
    psum x2 -> x0, blocking collectives: 32.8 us -> none  [the longest x1 30.3 us: local(): lax.psum((jnp.sum(residual * residual), jnp.sum(direction * image), jnp.s...]
    all_to_all x6 -> x0, starting transfers between devices: 25.1 us -> none  [the longest x1 6.93 us: local(): lax.all_to_all(obs_cell, 'tile', split_axis=0, concat_axis=0, tiled=True)]
    reduce_scatter x1 -> x0, waiting for transfers between devices: 16.3 us -> none  [local(): lax.psum_scatter(tile_adjoint.reshape(tile_field.shape), 'tm', scatter_di...]
  transfers between devices with their start and end apart: 39 -> 0, of which waited for: 26 -> 0; matrix products, arithmetic and copies ran while one was open for 15% -> 0% of each run, Pallas kernels for 0% -> 0%
where the time goes in v1:
time: 78 us; the launch traced here: 77.4 us
  Pallas kernels  65.9 us (84%)
  local copies, waits for them, and re-layouts  8.55 us (11%)
  other arithmetic  2.27 us (3%)
    pallas_call x1, Pallas kernels, local(): pl.pallas_call(functools.partial(kernel, sizes), out_shape=(jax.ShapeDtyp...  65.9 us
    unnamed x22, local copies, waits for them, and re-layouts  8 us
    add x1, other arithmetic, local(): updated_direction = residual_new + beta * direction  2.27 us

profile of v1, /device:TPU:0, one launch (start us, length us, event | category | flops | bytes accessed | tf_op | source)
XLA Modules:
  0.0 77.4 jit_solution(13819384713097134801)
XLA Ops:
  0.6 0.0 copy-start
  0.6 1.0 %copy-done = f32[8,8,1536]{2,1,0:T(8,128)S(1)} copy-done((f32[8,8,1536]{2,1,0:T(8,128)S(1)}, f32[8,8,1536]{2,1,0:T(8,128)}, u32[]{:S(2)}) %copy-start) | copy-done | bytes 393240
  1.6 0.0 copy-start.1
  1.6 1.0 %copy-done.1 = f32[8,8,1536]{2,1,0:T(8,128)S(1)} copy-done((f32[8,8,1536]{2,1,0:T(8,128)S(1)}, f32[8,8,1536]{2,1,0:T(8,128)}, u32[]{:S(2)}) %copy-start.1) | copy-done | bytes 393240
  2.6 0.0 copy-start.2
  2.6 1.0 %copy-done.2 = f32[8,8,1536]{2,1,0:T(8,128)S(1)} copy-done((f32[8,8,1536]{2,1,0:T(8,128)S(1)}, f32[8,8,1536]{2,1,0:T(8,128)}, u32[]{:S(2)}) %copy-start.2) | copy-done | bytes 393240
  3.6 0.0 copy-start.3
  3.6 0.8 %copy-done.3 = f32[4,4,8,128]{3,2,1,0:T(8,128)S(1)} copy-done((f32[4,4,8,128]{3,2,1,0:T(8,128)S(1)}, f32[4,4,8,128]{3,2,1,0:T(8,128)}, u32[]{:S(2)}) %copy-start.3) | copy-done | bytes 65560
  4.5 0.0 copy-start.4
  4.5 0.8 copy-done.4
  5.2 0.0 copy-start.5
  5.2 0.7 copy-done.5
  5.9 0.0 copy-start.6
  5.9 0.7 copy-done.6
  6.6 0.0 copy-start.7
  6.6 0.7 copy-done.7
  7.3 0.0 copy-start.8
  7.3 0.7 copy-done.8
  8.0 0.0 copy-start.9
  8.0 0.7 copy-done.9
  8.7 0.0 copy-start.10
  8.7 65.9 %shard_map.130 = (f32[8,8,1536]{2,1,0:T(8,128)S(1)}, f32[8,128]{1,0:T(8,128)S(1)}) custom-call(f32[8,8,1536]{2,1,0:T(8,128)S(1)} %copy-done.1, f32[8,8,1536]{2,1,0:T(8,128)S(1)} %copy-done, f32[8,8,1536]{2,1,0:T(8,128)S(1)} %copy-done.2, f32[8]{0:T(128)S(1)} %copy-done.9, s32[4,4,128]{2,1,0:T(4,128)S(1)} %copy-done.5, s32[4,4,128]{2,1,0:T(4,128)S(1)} %copy-done.6, ...), custom_call_target="tpu_custom_call" | custom-call | tf_op jit(solution)/shard_map/pallas_call | solution.py:380
  74.6 0.5 fusion
  75.2 0.0 copy-done.10
  75.2 2.3 %multiply_add_fusion = (f32[8,8,1536]{2,1,0:T(8,128)}, f32[8,8,1536]{2,1,0:T(8,128)}, f32[8,8,1536]{2,1,0:T(8,128)}) fusion(f32[8,8,1536]{2,1,0:T(8,128)S(1)} %copy-done, f32[]{:T(128)} %bitcast.1, f32[8,8,1536]{2,1,0:T(8,128)S(1)} %copy-done.1, f32[8,8,1536]{2,1,0:T(8,128)S(1)} %get-tuple-element.6, f32[]{:T(128)} %bitcast, f32[8,8,1536]{2,1,0:T(8,128)S(1)} %copy-done.10), kind=kLoop, calls=%fused_computation | loop fusion | flops 589824 | bytes 2752520 | tf_op jit(solution)/shard_map/add | solution.py:421
Async XLA Ops:
  0.6 1.0 %copy-start = (f32[8,8,1536]{2,1,0:T(8,128)S(1)}, f32[8,8,1536]{2,1,0:T(8,128)}, u32[]{:S(2)}) copy-start(f32[8,8,1536]{2,1,0:T(8,128)} %direction.1) | copy-start | bytes 1179652
  1.6 1.0 %copy-start.1 = (f32[8,8,1536]{2,1,0:T(8,128)S(1)}, f32[8,8,1536]{2,1,0:T(8,128)}, u32[]{:S(2)}) copy-start(f32[8,8,1536]{2,1,0:T(8,128)} %residual.1) | copy-start | bytes 1179652
  2.6 1.0 %copy-start.2 = (f32[8,8,1536]{2,1,0:T(8,128)S(1)}, f32[8,8,1536]{2,1,0:T(8,128)}, u32[]{:S(2)}) copy-start(f32[8,8,1536]{2,1,0:T(8,128)} %sigma.1) | copy-start | bytes 1179652
  3.6 0.8 %copy-start.3 = (f32[4,4,8,128]{3,2,1,0:T(8,128)S(1)}, f32[4,4,8,128]{3,2,1,0:T(8,128)}, u32[]{:S(2)}) copy-start(f32[4,4,8,128]{3,2,1,0:T(8,128)} %vert.1) | copy-start | bytes 196612
  4.5 0.8 copy-start.4
  5.2 0.7 copy-start.5
  5.9 0.7 copy-start.6
  6.6 0.7 copy-start.7
  7.3 0.7 copy-start.8
  8.0 0.7 copy-start.9
  8.7 66.5 %copy-start.10 = (f32[8,8,1536]{2,1,0:T(8,128)S(1)}, f32[8,8,1536]{2,1,0:T(8,128)}, u32[]{:S(2)}) copy-start(f32[8,8,1536]{2,1,0:T(8,128)} %param.11) | copy-start | bytes 1179652

commit v2 on v1

--- a/solution.py
+++ b/solution.py
@@ -24,8 +24,9 @@
 
 def kernel(
     sizes,
-    residual, direction, sigma, decay, cell, slot, count, horiz, vert, prec,
+    residual_h, direction_h, sigma_h, decay, cell_h, slot_h, count, horiz_h, vert_h, prec_h,
     image, scal,
+    residual, direction, sigma, cell, slot, horiz, vert, prec, onehots, load_sem,
     a0, a1, t0, t1, top, bot, rd, ru, xd, xu, xc, pack, obs, fields, parts, models,
     acc, ip1, ip2,
     halo_send, halo_recv, obs_send, obs_recv, mod_send, mod_recv,
@@ -35,6 +36,7 @@
     levels, rows, width = direction.shape
     blocks = cell.shape[1]
     ng, ngroup = nt * ntm, ntm * nlev
+    keep = onehots.shape[0] > 1
     member = lax.axis_index("member")
     tile = lax.axis_index("tile")
     tm = lax.axis_index("tm")
@@ -46,6 +48,18 @@
     def dev(index, level):
         return (member, index // ntm, lax.rem(index, ntm), level)
 
+    loads = [
+        pltpu.make_async_copy(src, dst, load_sem.at[n])
+        for n, (src, dst) in enumerate(
+            [
+                (direction_h, direction), (vert_h, vert), (horiz_h, horiz), (cell_h, cell),
+                (slot_h, slot), (prec_h, prec), (sigma_h, sigma), (residual_h, residual),
+            ]
+        )
+    ]
+    for load in loads:
+        load.start()
+
     barrier = pltpu.get_barrier_semaphore()
     everyone = ng * nlev
     me = g * nlev + lev
@@ -71,9 +85,9 @@
         plan = [
             (top, rd.at[phase], up, lev, has_up, has_down),
             (bot, ru.at[phase], down, lev, has_down, has_up),
-            (top.at[half], xd.at[phase], up, other, has_up, has_down),
-            (bot.at[half], xu.at[phase], down, other, has_down, has_up),
             (source.at[edge], xc.at[phase], g, other, None, None),
+            (rd.at[phase].at[half], xd.at[phase], g, other, has_down, has_down),
+            (ru.at[phase].at[half], xu.at[phase], g, other, has_up, has_up),
         ]
         return [
             (
@@ -93,11 +107,10 @@
         else:
             pl.when(condition)(action)
 
+    loads[0].wait()
     pack_rows(direction, 0)
-    pl.semaphore_wait(barrier, everyone - 1)
-    halo1 = halo_copies(0, direction, 0)
-    for copy, sends, gets in halo1:
-        when(sends, copy.start)
+    for load in loads[1:6]:
+        load.wait()
 
     eff_rows = blocks * levels
     h_rows = eff_rows + blocks * 4
@@ -119,6 +132,10 @@
         return carry
 
     lax.fori_loop(0, nt, pack_tile, 0)
+    pl.semaphore_wait(barrier, everyone - 1)
+    halo1 = halo_copies(0, direction, 0)
+    for copy, sends, gets in halo1[:3]:
+        when(sends, copy.start)
 
     def obs_copy(i):
         to = lax.rem(g + i, ng)
@@ -156,9 +173,12 @@
     far = 1 + levels * other
 
     def receive(phase, copies):
-        for copy, sends, gets in copies:
+        for n in range(2):
+            when(copies[n][2], copies[n][0].wait_recv)
+            when(copies[3 + n][1], copies[3 + n][0].start)
+        unpack(rd.at[phase], ru.at[phase], levels // 2, own)
+        for copy, sends, gets in copies[2:]:
             when(gets, copy.wait_recv)
-        unpack(rd.at[phase], ru.at[phase], levels // 2, own)
         unpack(xd.at[phase], xu.at[phase], HALO // 2, far)
         for l in range(HALO):
             a0[far + l] = xc[phase, l]
@@ -192,6 +212,7 @@
     receive(0, halo1)
     smooth()
 
+    loads[6].wait()
     cells_here = levels * rows
     increment = (sigma[...] * a0[pl.ds(own, levels)]).reshape(cells_here, width)
     high, low = split(increment)
@@ -224,12 +245,17 @@
             + jnp.where(upper, lanes(q, eff_rows + 2 + k, 4), 0.0)
             for k in range(2)
         ]
+        return weights, col
+
+    def matrix(col):
         col_id = lax.broadcasted_iota(jnp.int32, (width, nobs), 0)
-        onehot = jnp.where(col_id == col, 1.0, 0.0).astype(bf16)
-        return weights, onehot
+        return jnp.where(col_id == col, 1.0, 0.0).astype(bf16)
 
     def gather(q, carry):
-        weights, onehot = stencil(q)
+        weights, col = stencil(q)
+        onehot = matrix(col)
+        if keep:
+            onehots[q] = onehot
         values = jnp.dot(fields[...], onehot, preferred_element_type=f32)
         values = values[: 2 * cells_here] + values[2 * cells_here :]
         total = jnp.zeros((rows, nobs), f32)
@@ -272,7 +298,8 @@
         back.wait_recv()
 
     def scatter(q, carry):
-        weights, onehot = stencil(q)
+        weights, col = stencil(q)
+        onehot = onehots[q] if keep else matrix(col)
         model = models[0, q]
         for k in range(1, ngroup):
             model = model + models[k, q]
@@ -294,11 +321,12 @@
     a0[pl.ds(own, levels)] = sigma[...] * adjoint.reshape(levels, rows, width)
     pack_rows(a0, own)
     halo2 = halo_copies(1, a0, own)
-    for copy, sends, gets in halo2:
+    for copy, sends, gets in halo2[:3]:
         when(sends, copy.start)
     receive(1, halo2)
     smooth()
 
+    loads[7].wait()
     sums = [jnp.zeros((rows, width), f32)] * 4
     for l in range(levels):
         d, r = direction[l], residual[l]
@@ -374,6 +402,8 @@
     ng, ngroup = nt * ntm, ntm * nlev
     packed = blocks * (levels + 6)
     vmem = pl.BlockSpec(memory_space=pltpu.VMEM)
+    hbm = pl.BlockSpec(memory_space=pl.ANY)
+    matrices = ng if ng * width * blocks * 128 <= 2**23 else 1
     smem = pl.BlockSpec(memory_space=pltpu.SMEM)
     field = pltpu.VMEM((levels + HALO + 2, rows, width), f32)
     dma = pltpu.SemaphoreType.DMA
@@ -383,9 +413,18 @@
             jax.ShapeDtypeStruct((levels, rows, width), f32),
             jax.ShapeDtypeStruct((8, 128), f32),
         ),
-        in_specs=[vmem, vmem, vmem, smem, vmem, vmem, smem, vmem, vmem, vmem],
+        in_specs=[hbm, hbm, hbm, smem, hbm, hbm, smem, hbm, hbm, hbm],
         out_specs=(vmem, vmem),
         scratch_shapes=[
+            *(
+                pltpu.VMEM(x.shape, x.dtype)
+                for x in (
+                    residual, direction, sigma, obs_cell, observation_slot,
+                    horiz_weight, vert_weight, obs_precision,
+                )
+            ),
+            pltpu.VMEM((matrices, width, blocks * 128), bf16),
+            pltpu.SemaphoreType.DMA((8,)),
             field, field, field, field,
             pltpu.VMEM((levels // 2, rows, width), f32),
             pltpu.VMEM((levels // 2, rows, width), f32),
@@ -409,7 +448,7 @@
             dma((nt,)), dma((nt,)),
         ],
         compiler_params=pltpu.CompilerParams(
-            collective_id=0, has_side_effects=True, vmem_limit_bytes=48 * 1024 * 1024
+            collective_id=0, has_side_effects=True, vmem_limit_bytes=60 * 1024 * 1024
         ),
     )(
         residual, direction, sigma, decay_rate, obs_cell, observation_slot, block_count,

time: 78 us -> 68.1 us (0.87)
  local copies, waits for them, and re-layouts: 8.55 us -> 1.36 us
  Pallas kernels: 65.9 us -> 62.4 us
  other arithmetic: 2.27 us -> 3.38 us
    unnamed x22 -> x6, local copies, waits for them, and re-layouts: 8 us -> 0.01 us
    pallas_call x1, Pallas kernels: 65.9 us -> 62.4 us  [local(): pl.pallas_call(functools.partial(kernel, sizes), out_shape=(jax.ShapeDtyp...]
    add x1, other arithmetic: 2.27 us -> 3.38 us  [local(): updated_direction = residual_new + beta * direction]
    slice x1, local copies, waits for them, and re-layouts: 0.55 us -> 1.35 us  [local(): alpha, beta = (scal[0, 0], scal[1, 0])]
where the time goes in v2:
time: 68.1 us; the launch traced here: 67.8 us
  Pallas kernels  62.4 us (92%)
  other arithmetic  3.38 us (5%)
  local copies, waits for them, and re-layouts  1.36 us (2%)
    pallas_call x1, Pallas kernels, local(): pl.pallas_call(functools.partial(kernel, sizes), out_shape=(jax.ShapeDtyp...  62.4 us
    add x1, other arithmetic, local(): updated_direction = residual_new + beta * direction  3.38 us

profile of v2, /device:TPU:0, one launch (start us, length us, event | category | flops | bytes accessed | tf_op | source)
XLA Modules:
  0.0 67.8 jit_solution(1245465465533465814)
XLA Ops:
  0.6 0.0 copy-start
  0.6 0.0 copy-start.1
  0.7 0.0 copy-start.2
  0.7 62.4 %shard_map.130 = (f32[8,8,1536]{2,1,0:T(8,128)}, f32[8,128]{1,0:T(8,128)}) custom-call(f32[8,8,1536]{2,1,0:T(8,128)} %residual_h.1, f32[8,8,1536]{2,1,0:T(8,128)} %direction_h.1, f32[8,8,1536]{2,1,0:T(8,128)} %sigma_h.1, f32[8]{0:T(128)} %decay.1, s32[4,4,128]{2,1,0:T(4,128)} %cell_h.1, s32[4,4,128]{2,1,0:T(4,128)} %slot_h.1, s32[4,4]{1,0:T(4,128)} %count.1, ...), custom_call_target="tpu_custom_call" | custom-call | tf_op jit(solution)/shard_map/pallas_call | solution.py:410
  63.1 1.4 %fusion = (f32[1,1]{1,0:T(1,128)}, f32[1,1]{1,0:T(1,128)}) fusion(f32[8,128]{1,0:T(8,128)} %get-tuple-element.5), kind=kLoop, calls=%fused_computation.3 | loop fusion | bytes 16 | tf_op jit(solution)/shard_map/slice | solution.py:457
  64.4 0.0 copy-done
  64.4 0.0 copy-done.1
  64.4 0.0 copy-done.2
  64.4 3.4 %multiply_add_fusion = (f32[8,8,1536]{2,1,0:T(8,128)}, f32[8,8,1536]{2,1,0:T(8,128)}, f32[8,8,1536]{2,1,0:T(8,128)}) fusion(f32[8,8,1536]{2,1,0:T(8,128)S(1)} %copy-done, f32[]{:T(128)} %bitcast.1, f32[8,8,1536]{2,1,0:T(8,128)S(1)} %copy-done.1, f32[8,8,1536]{2,1,0:T(8,128)} %get-tuple-element.6, f32[]{:T(128)} %bitcast, f32[8,8,1536]{2,1,0:T(8,128)S(1)} %copy-done.2), kind=kLoop, calls=%fused_computation | loop fusion | flops 589824 | bytes 2752520 | tf_op jit(solution)/shard_map/add | solution.py:460
Async XLA Ops:
  0.6 63.8 %copy-start = (f32[8,8,1536]{2,1,0:T(8,128)S(1)}, f32[8,8,1536]{2,1,0:T(8,128)}, u32[]{:S(2)}) copy-start(f32[8,8,1536]{2,1,0:T(8,128)} %direction_h.1) | copy-start | bytes 1179652
  0.6 63.8 %copy-start.1 = (f32[8,8,1536]{2,1,0:T(8,128)S(1)}, f32[8,8,1536]{2,1,0:T(8,128)}, u32[]{:S(2)}) copy-start(f32[8,8,1536]{2,1,0:T(8,128)} %residual_h.1) | copy-start | bytes 1179652
  0.7 63.8 %copy-start.2 = (f32[8,8,1536]{2,1,0:T(8,128)S(1)}, f32[8,8,1536]{2,1,0:T(8,128)}, u32[]{:S(2)}) copy-start(f32[8,8,1536]{2,1,0:T(8,128)} %param.11) | copy-start | bytes 1179652

commit v3 on v2

--- a/solution.py
+++ b/solution.py
@@ -28,9 +28,9 @@
     image, scal,
     residual, direction, sigma, cell, slot, horiz, vert, prec, onehots, load_sem,
     a0, a1, t0, t1, top, bot, rd, ru, xd, xu, xc, pack, obs, fields, parts, models,
-    acc, ip1, ip2,
+    acc, ip1,
     halo_send, halo_recv, obs_send, obs_recv, mod_send, mod_recv,
-    s1_send, s1_recv, s2_send, s2_recv,
+    s1_send, s1_recv,
 ):
     nt, ntm, nlev = sizes
     levels, rows, width = direction.shape
@@ -78,13 +78,18 @@
             top[j] = jnp.where(low_half, even, odd)
             bot[j] = jnp.where(low_half, odd, even)
 
+    pairs = levels // 2
+
     def halo_copies(phase, source, base):
         up, down = g - 1, g + 1
         half = pl.ds(2 * other, 2)
         edge = pl.ds(base + HALO * other, HALO)
-        plan = [
-            (top, rd.at[phase], up, lev, has_up, has_down),
-            (bot, ru.at[phase], down, lev, has_down, has_up),
+        plan = []
+        for c in range(pairs):
+            j = c + lev * (pairs - 1 - 2 * c)
+            plan.append((top.at[j], rd.at[phase, j], up, lev, has_up, has_down))
+            plan.append((bot.at[j], ru.at[phase, j], down, lev, has_down, has_up))
+        plan += [
             (source.at[edge], xc.at[phase], g, other, None, None),
             (rd.at[phase].at[half], xd.at[phase], g, other, has_down, has_down),
             (ru.at[phase].at[half], xu.at[phase], g, other, has_up, has_up),
@@ -134,7 +139,7 @@
     lax.fori_loop(0, nt, pack_tile, 0)
     pl.semaphore_wait(barrier, everyone - 1)
     halo1 = halo_copies(0, direction, 0)
-    for copy, sends, gets in halo1[:3]:
+    for copy, sends, gets in halo1[: 2 * pairs + 1]:
         when(sends, copy.start)
 
     def obs_copy(i):
@@ -158,12 +163,11 @@
 
     inside = (low_half & has_down) | (jnp.logical_not(low_half) & has_up)
 
-    def unpack(down, up, n, base):
-        for j in range(n):
-            a1[base + 2 * j] = jnp.where(inside, jnp.where(low_half, down[j], up[j]), 0.0)
-            a1[base + 2 * j + 1] = jnp.where(
-                inside, pltpu.roll(jnp.where(low_half, up[j], down[j]), HALO, 0), 0.0
-            )
+    def unpack(down, up, at):
+        a1[at] = jnp.where(inside, jnp.where(low_half, down, up), 0.0)
+        a1[at + 1] = jnp.where(
+            inside, pltpu.roll(jnp.where(low_half, up, down), HALO, 0), 0.0
+        )
 
     zero = jnp.zeros((rows, width), f32)
     for buffer in (a0, a1, t0, t1):
@@ -172,45 +176,55 @@
     own = 1 + HALO * lev
     far = 1 + levels * other
 
-    def receive(phase, copies):
-        for n in range(2):
-            when(copies[n][2], copies[n][0].wait_recv)
-            when(copies[3 + n][1], copies[3 + n][0].start)
-        unpack(rd.at[phase], ru.at[phase], levels // 2, own)
-        for copy, sends, gets in copies[2:]:
+    def advance(step, w, src0, src1, dst0, dst1):
+        place = w - step
+        l = 1 + place + lev * (levels + HALO - 1 - 2 * place)
+        full = jnp.concatenate([src0[l], src1[l]], axis=0)
+        near = (
+            pltpu.roll(full, 1, 0) + pltpu.roll(full, 2 * rows - 1, 0)
+            + pltpu.roll(full, 1, 1) + pltpu.roll(full, width - 1, 1)
+        )
+        main = center_coef * full + row_coef * near
+        dst0[l] = main[:rows] + level_coef * (src0[l - 1] + src0[l + 1])
+        if step < K_DIFF:
+            side = main[rows:] + level_coef * (src1[l - 1] + src1[l + 1])
+            dst1[l] = jnp.where(inside, side, 0.0)
+
+    def wave(start, end):
+        def body(w, carry):
+            for step in range(1, K_DIFF + 1):
+                to = (t0, t1) if step % 2 else (a0, a1)
+                of = (a0, a1) if step % 2 else (t0, t1)
+                pl.when(w >= step)(functools.partial(advance, step, w, *of, *to))
+            return carry
+
+        lax.fori_loop(start, end, body, 0)
+
+    def smooth(phase, copies):
+        for c in range(pairs):
+            j = c + lev * (pairs - 1 - 2 * c)
+            for n in range(2):
+                when(copies[2 * c + n][2], copies[2 * c + n][0].wait_recv)
+            if c == pairs - 1:
+                for n in range(2):
+                    forward = copies[2 * pairs + 1 + n]
+                    when(forward[1], forward[0].start)
+            unpack(rd[phase, j], ru[phase, j], own + 2 * j)
+            if c == 0:
+                copies[2 * pairs][0].wait()
+            wave(max(1, 2 * c), 2 * c + 2)
+        for copy, sends, gets in copies[2 * pairs + 1 :]:
             when(gets, copy.wait_recv)
-        unpack(xd.at[phase], xu.at[phase], HALO // 2, far)
+        for j in range(HALO // 2):
+            unpack(xd[phase, j], xu[phase, j], far + 2 * j)
         for l in range(HALO):
             a0[far + l] = xc[phase, l]
-        for copy, sends, gets in copies:
+        wave(levels, levels + HALO)
+        for copy, sends, gets in copies[: 2 * pairs] + copies[2 * pairs + 1 :]:
             when(sends, copy.wait_send)
 
-    def smooth_step(step, src0, src1, dst0, dst1):
-        def body(i, carry):
-            l = 1 + step * lev + i
-            full = jnp.concatenate([src0[l], src1[l]], axis=0)
-            near = (
-                pltpu.roll(full, 1, 0) + pltpu.roll(full, 2 * rows - 1, 0)
-                + pltpu.roll(full, 1, 1) + pltpu.roll(full, width - 1, 1)
-            )
-            main = center_coef * full + row_coef * near
-            dst0[l] = main[:rows] + level_coef * (src0[l - 1] + src0[l + 1])
-            if step < K_DIFF:
-                side = main[rows:] + level_coef * (src1[l - 1] + src1[l + 1])
-                dst1[l] = jnp.where(inside, side, 0.0)
-            return carry
-
-        lax.fori_loop(0, levels + HALO - step, body, 0)
-
-    def smooth():
-        smooth_step(1, a0, a1, t0, t1)
-        smooth_step(2, t0, t1, a0, a1)
-        smooth_step(3, a0, a1, t0, t1)
-        smooth_step(4, t0, t1, a0, a1)
-
     a0[pl.ds(own, levels)] = direction[...]
-    receive(0, halo1)
-    smooth()
+    smooth(0, halo1)
 
     loads[6].wait()
     cells_here = levels * rows
@@ -321,10 +335,9 @@
     a0[pl.ds(own, levels)] = sigma[...] * adjoint.reshape(levels, rows, width)
     pack_rows(a0, own)
     halo2 = halo_copies(1, a0, own)
-    for copy, sends, gets in halo2[:3]:
+    for copy, sends, gets in halo2[: 2 * pairs + 1]:
         when(sends, copy.start)
-    receive(1, halo2)
-    smooth()
+    smooth(1, halo2)
 
     loads[7].wait()
     sums = [jnp.zeros((rows, width), f32)] * 4
@@ -341,35 +354,25 @@
         for at in range(128, width, 128):
             line = line + total[:, at : at + 128]
         lines.append(line)
-    ip1[tg] = jnp.concatenate(lines + [jnp.zeros((4, 128), f32)], axis=0)
-    swaps1 = [exchange(i, ip1.at[tg], ip1, s1_send, s1_recv) for i in range(1, ngroup)]
+    ip1[me] = jnp.concatenate(lines + [jnp.zeros((4, 128), f32)], axis=0)
+    swaps1 = []
+    for i in range(1, everyone):
+        to = lax.rem(me + i, everyone)
+        swaps1.append(
+            [
+                pltpu.make_async_remote_copy(
+                    src_ref=ip1.at[me], dst_ref=ip1.at[at],
+                    send_sem=s1_send.at[i], recv_sem=s1_recv.at[i],
+                    device_id=dev(to // nlev, lax.rem(to, nlev)), device_id_type=MESH,
+                )
+                for at in (me, lax.rem(me - i + everyone, everyone))
+            ]
+        )
     for out, _ in swaps1:
         out.start()
     for _, back in swaps1:
         back.wait_recv()
-    total = ip1[0]
-    for k in range(1, ngroup):
-        total = total + ip1[k]
-    ip2[tile] = total
-    swaps2 = []
-    for i in range(1, nt):
-        swaps2.append(
-            [
-                pltpu.make_async_remote_copy(
-                    src_ref=ip2.at[tile], dst_ref=ip2.at[at],
-                    send_sem=s2_send.at[i], recv_sem=s2_recv.at[i],
-                    device_id=(member, lax.rem(tile + i, nt), tm, lev), device_id_type=MESH,
-                )
-                for at in (tile, lax.rem(tile - i + nt, nt))
-            ]
-        )
-    for out, _ in swaps2:
-        out.start()
-    for _, back in swaps2:
-        back.wait_recv()
-    total = ip2[0]
-    for k in range(1, nt):
-        total = total + ip2[k]
+    total = jnp.sum(ip1[...], axis=0)
     total = jnp.broadcast_to(jnp.sum(total, axis=1, keepdims=True), (8, 128))
     norm_old, curvature, cross, image_norm = (total[n : n + 1] for n in range(4))
     alpha = norm_old / curvature
@@ -378,7 +381,7 @@
 
     for i in range(1, ng):
         obs_copy(i).wait_send()
-    for out, _ in swaps + swaps1 + swaps2:
+    for out, _ in swaps + swaps1:
         out.wait_send()
 
 
@@ -439,13 +442,11 @@
             pltpu.VMEM((ng, 8, 128), f32),
             pltpu.VMEM((ngroup, ng, 8, 128), f32),
             pltpu.VMEM((4 * levels * rows, width), f32),
-            pltpu.VMEM((ngroup, 8, 128), f32),
-            pltpu.VMEM((nt, 8, 128), f32),
-            dma((2, 5)), dma((2, 5)),
+            pltpu.VMEM((ng * nlev, 8, 128), f32),
+            dma((2, levels + 3)), dma((2, levels + 3)),
             dma((ng,)), dma((ng,)),
             dma((ngroup,)), dma((ngroup,)),
-            dma((ngroup,)), dma((ngroup,)),
-            dma((nt,)), dma((nt,)),
+            dma((ng * nlev,)), dma((ng * nlev,)),
         ],
         compiler_params=pltpu.CompilerParams(
             collective_id=0, has_side_effects=True, vmem_limit_bytes=60 * 1024 * 1024

time: 68.1 us -> 61.5 us (0.903)
  Pallas kernels: 62.4 us -> 55.8 us
    pallas_call x1, Pallas kernels: 62.4 us -> 55.8 us  [local(): pl.pallas_call(functools.partial(kernel, sizes), out_shape=(jax.ShapeDtyp...]
where the time goes in v3:
time: 61.5 us; the launch traced here: 61.3 us
  Pallas kernels  55.8 us (91%)
  other arithmetic  3.38 us (5%)
  local copies, waits for them, and re-layouts  1.36 us (2%)
  between operations  0.67 us (1%)
    pallas_call x1, Pallas kernels, local(): pl.pallas_call(functools.partial(kernel, sizes), out_shape=(jax.ShapeDtyp...  55.8 us
    add x1, other arithmetic, local(): updated_direction = residual_new + beta * direction  3.38 us
    slice x1, local copies, waits for them, and re-layouts, local(): alpha, beta = (scal[0, 0], scal[1, 0])  1.35 us

profile of v3, /device:TPU:0, one launch (start us, length us, event | category | flops | bytes accessed | tf_op | source)
XLA Modules:
  0.0 61.3 jit_solution(225024292403819332)
XLA Ops:
  0.6 0.0 copy-start
  0.6 0.0 copy-start.1
  0.7 0.0 copy-start.2
  0.7 55.8 %shard_map.130 = (f32[8,8,1536]{2,1,0:T(8,128)}, f32[8,128]{1,0:T(8,128)}) custom-call(f32[8,8,1536]{2,1,0:T(8,128)} %residual_h.1, f32[8,8,1536]{2,1,0:T(8,128)} %direction_h.1, f32[8,8,1536]{2,1,0:T(8,128)} %sigma_h.1, f32[8]{0:T(128)} %decay.1, s32[4,4,128]{2,1,0:T(4,128)} %cell_h.1, s32[4,4,128]{2,1,0:T(4,128)} %slot_h.1, s32[4,4]{1,0:T(4,128)} %count.1, ...), custom_call_target="tpu_custom_call" | custom-call | tf_op jit(solution)/shard_map/pallas_call | solution.py:413
  56.5 1.4 %fusion = (f32[1,1]{1,0:T(1,128)}, f32[1,1]{1,0:T(1,128)}) fusion(f32[8,128]{1,0:T(8,128)} %get-tuple-element.5), kind=kLoop, calls=%fused_computation.3 | loop fusion | bytes 16 | tf_op jit(solution)/shard_map/slice | solution.py:458
  57.9 0.0 copy-done
  57.9 0.0 copy-done.1
  57.9 0.0 copy-done.2
  57.9 3.4 %multiply_add_fusion = (f32[8,8,1536]{2,1,0:T(8,128)}, f32[8,8,1536]{2,1,0:T(8,128)}, f32[8,8,1536]{2,1,0:T(8,128)}) fusion(f32[8,8,1536]{2,1,0:T(8,128)S(1)} %copy-done, f32[]{:T(128)} %bitcast.1, f32[8,8,1536]{2,1,0:T(8,128)S(1)} %copy-done.1, f32[8,8,1536]{2,1,0:T(8,128)} %get-tuple-element.6, f32[]{:T(128)} %bitcast, f32[8,8,1536]{2,1,0:T(8,128)S(1)} %copy-done.2), kind=kLoop, calls=%fused_computation | loop fusion | flops 589824 | bytes 2752520 | tf_op jit(solution)/shard_map/add | solution.py:461
Async XLA Ops:
  0.6 57.2 %copy-start = (f32[8,8,1536]{2,1,0:T(8,128)S(1)}, f32[8,8,1536]{2,1,0:T(8,128)}, u32[]{:S(2)}) copy-start(f32[8,8,1536]{2,1,0:T(8,128)} %direction_h.1) | copy-start | bytes 1179652
  0.6 57.2 %copy-start.1 = (f32[8,8,1536]{2,1,0:T(8,128)S(1)}, f32[8,8,1536]{2,1,0:T(8,128)}, u32[]{:S(2)}) copy-start(f32[8,8,1536]{2,1,0:T(8,128)} %residual_h.1) | copy-start | bytes 1179652
  0.7 57.2 %copy-start.2 = (f32[8,8,1536]{2,1,0:T(8,128)S(1)}, f32[8,8,1536]{2,1,0:T(8,128)}, u32[]{:S(2)}) copy-start(f32[8,8,1536]{2,1,0:T(8,128)} %param.11) | copy-start | bytes 1179652

commit v4 on v3

--- a/solution.py
+++ b/solution.py
@@ -330,13 +330,22 @@
         return carry
 
     lax.fori_loop(0, ng, scatter, 0)
-    adjoint = acc[: 2 * cells_here] + acc[2 * cells_here :]
-    adjoint = adjoint[:cells_here] + pltpu.roll(adjoint[cells_here:], 1, 1)
-    a0[pl.ds(own, levels)] = sigma[...] * adjoint.reshape(levels, rows, width)
-    pack_rows(a0, own)
     halo2 = halo_copies(1, a0, own)
-    for copy, sends, gets in halo2[: 2 * pairs + 1]:
-        when(sends, copy.start)
+    for c in range(pairs):
+        j = c + lev * (pairs - 1 - 2 * c)
+        for n in range(2):
+            l = 2 * j + n
+            quarters = [
+                acc[pl.ds(pl.multiple_of(k * cells_here + l * rows, rows), rows)] for k in range(4)
+            ]
+            shifted = pltpu.roll(quarters[1] + quarters[3], 1, 1)
+            a0[own + l] = sigma[l] * (quarters[0] + quarters[2] + shifted)
+        even, odd = a0[own + 2 * j], pltpu.roll(a0[own + 2 * j + 1], HALO, 0)
+        top[j] = jnp.where(low_half, even, odd)
+        bot[j] = jnp.where(low_half, odd, even)
+        for copy, sends, gets in halo2[2 * c : 2 * c + 2]:
+            when(sends, copy.start)
+    halo2[2 * pairs][0].start()
     smooth(1, halo2)
 
     loads[7].wait()

time: 61.5 us -> 61.4 us (level)
  no operation moved by 1% of the time
where the time goes in v4:
time: 61.4 us; the launch traced here: 61.1 us
  Pallas kernels  55.7 us (91%)
  other arithmetic  3.38 us (6%)
  local copies, waits for them, and re-layouts  1.36 us (2%)
  between operations  0.67 us (1%)
    pallas_call x1, Pallas kernels, local(): pl.pallas_call(functools.partial(kernel, sizes), out_shape=(jax.ShapeDtyp...  55.7 us
    add x1, other arithmetic, local(): updated_direction = residual_new + beta * direction  3.38 us
    slice x1, local copies, waits for them, and re-layouts, local(): alpha, beta = (scal[0, 0], scal[1, 0])  1.35 us

profile of v4, /device:TPU:0, one launch (start us, length us, event | category | flops | bytes accessed | tf_op | source)
XLA Modules:
  0.0 61.1 jit_solution(7988178252279588919)
XLA Ops:
  0.6 0.0 copy-start
  0.6 0.0 copy-start.1
  0.7 0.0 copy-start.2
  0.7 55.7 %shard_map.130 = (f32[8,8,1536]{2,1,0:T(8,128)}, f32[8,128]{1,0:T(8,128)}) custom-call(f32[8,8,1536]{2,1,0:T(8,128)} %residual_h.1, f32[8,8,1536]{2,1,0:T(8,128)} %direction_h.1, f32[8,8,1536]{2,1,0:T(8,128)} %sigma_h.1, f32[8]{0:T(128)} %decay.1, s32[4,4,128]{2,1,0:T(4,128)} %cell_h.1, s32[4,4,128]{2,1,0:T(4,128)} %slot_h.1, s32[4,4]{1,0:T(4,128)} %count.1, ...), custom_call_target="tpu_custom_call" | custom-call | tf_op jit(solution)/shard_map/pallas_call | solution.py:422
  56.4 1.4 %fusion = (f32[1,1]{1,0:T(1,128)}, f32[1,1]{1,0:T(1,128)}) fusion(f32[8,128]{1,0:T(8,128)} %get-tuple-element.5), kind=kLoop, calls=%fused_computation.3 | loop fusion | bytes 16 | tf_op jit(solution)/shard_map/slice | solution.py:467
  57.7 0.0 copy-done
  57.7 0.0 copy-done.1
  57.7 0.0 copy-done.2
  57.7 3.4 %multiply_add_fusion = (f32[8,8,1536]{2,1,0:T(8,128)}, f32[8,8,1536]{2,1,0:T(8,128)}, f32[8,8,1536]{2,1,0:T(8,128)}) fusion(f32[8,8,1536]{2,1,0:T(8,128)S(1)} %copy-done, f32[]{:T(128)} %bitcast.1, f32[8,8,1536]{2,1,0:T(8,128)S(1)} %copy-done.1, f32[8,8,1536]{2,1,0:T(8,128)} %get-tuple-element.6, f32[]{:T(128)} %bitcast, f32[8,8,1536]{2,1,0:T(8,128)S(1)} %copy-done.2), kind=kLoop, calls=%fused_computation | loop fusion | flops 589824 | bytes 2752520 | tf_op jit(solution)/shard_map/add | solution.py:470
Async XLA Ops:
  0.6 57.1 %copy-start = (f32[8,8,1536]{2,1,0:T(8,128)S(1)}, f32[8,8,1536]{2,1,0:T(8,128)}, u32[]{:S(2)}) copy-start(f32[8,8,1536]{2,1,0:T(8,128)} %direction_h.1) | copy-start | bytes 1179652
  0.6 57.1 %copy-start.1 = (f32[8,8,1536]{2,1,0:T(8,128)S(1)}, f32[8,8,1536]{2,1,0:T(8,128)}, u32[]{:S(2)}) copy-start(f32[8,8,1536]{2,1,0:T(8,128)} %residual_h.1) | copy-start | bytes 1179652
  0.7 57.1 %copy-start.2 = (f32[8,8,1536]{2,1,0:T(8,128)S(1)}, f32[8,8,1536]{2,1,0:T(8,128)}, u32[]{:S(2)}) copy-start(f32[8,8,1536]{2,1,0:T(8,128)} %param.11) | copy-start | bytes 1179652
